TPU v7x, 512 devices: a whole 4x8x8 slice. The times are simulated.
512 devices in a mesh: dp: 32 (over x, y), tp: 16 (over z, core).
Axes of the slice: x: 4, y: 8, z: 8, core: 2. Of those that a mesh axis runs over, the one named last changes fastest.
Arguments:
- embeddings: bfloat16 [12288, 192, 256], P(('dp', 'tp')), may hold values from -6 to 6
- projection: bfloat16 [256, 16], replicated, may hold values from -0.375 to 0.375
- compress: bfloat16 [256, 4], replicated, may hold values from -0.375 to 0.375
- w_up: bfloat16 [4096, 4096], P(None, 'tp'), may hold values from -0.09375 to 0.09375
- w_down: bfloat16 [4096, 768], P('tp'), may hold values from -0.125 to 0.125
- output_norm_gain: float32 [1536], P('tp'), may hold values from 0.25 to 1.75
- out_grad: bfloat16 [12288, 1536], P('dp', 'tp'), may hold values from -6 to 6
Outputs:
- block_result: bfloat16 [12288, 1536], P('dp', 'tp')
- grad_down: float32 [4096, 768], P(('tp', 'dp'))
All inputs are finite; a program needn't handle non-finite values.
Results may differ from a plain program's by a relative error of at most 0.017.
Values may be sent and summed in bfloat16 or wider, within the bound.
No kernel may reach another device: no remote copies, remote signals or barrier semaphores. Data moves between devices by JAX's collectives and lax.ppermute only.
A program may use at most 64 MiB of HBM per device.

v0:
```python
import jax
import jax.numpy as jnp
from jax import lax
from jax.sharding import PartitionSpec as P

BF16, F16, F32 = (jnp.bfloat16, jnp.float16, jnp.float32)
NORMED_SCALE, LCB_SCALE, GG_SCALE = (512.0, 64.0, 4096.0)


def high_low(x):
    high = lax.reduce_precision(x, 8, 7)
    return (high.astype(BF16), (x - high).astype(BF16))


def on_device(embeddings, projection, compress, w_up, w_down, output_norm_gain, out_grad):
    samples, edim, fields = embeddings.shape
    tp = lax.axis_size("tp")
    dp = lax.axis_size("dp")
    me = lax.axis_index("tp")
    core = me % 2
    group_rows = samples * tp
    feat, fmw = (w_up.shape[0], w_down.shape[1])
    own = fmw // tp
    width = 2 * own
    pairs = jnp.einsum("sef,fk->sek", embeddings, projection, preferred_element_type=F32).astype(
        BF16
    )
    inter = jnp.einsum("sek,sef->skf", pairs, embeddings, preferred_element_type=F32).reshape(
        samples, -1
    )
    center = inter - jnp.mean(inter, axis=1, keepdims=True)
    spread = jnp.mean(center * center, axis=1, keepdims=True)
    normed = (center * (NORMED_SCALE / jnp.sqrt(spread + 1e-05))).astype(F16)
    lcb = jnp.einsum("sef,fj->sje", embeddings, compress, preferred_element_type=F32).reshape(
        samples, -1
    )
    gg = out_grad.T.astype(F32) * output_norm_gain[:, None]
    gg_packed = (
        (gg[:own] * GG_SCALE)
        .astype(F16)
        .reshape(3, 2, 8, group_rows)
        .transpose(0, 2, 1, 3)
        .reshape(samples, -1)
    )
    sent = jnp.concatenate([normed, (lcb * LCB_SCALE).astype(F16), gg_packed], axis=1)
    got = lax.all_gather(sent, "tp", axis=0, tiled=True)
    pre = jnp.dot(got[:, :feat].astype(BF16), w_up, preferred_element_type=F32)
    hidden = jax.nn.gelu(pre * (1.0 / NORMED_SCALE), approximate=True).astype(BF16)
    mlp = jnp.einsum("hc,sh->cs", w_down, hidden, preferred_element_type=F32)
    mlp = mlp.reshape(tp // 2, 2, own, group_rows)
    swap = [(i, i ^ 1) for i in range(tp)]
    theirs = lax.dynamic_index_in_dim(mlp, 1 - core, 1, keepdims=False).astype(BF16)
    mine = lax.dynamic_index_in_dim(mlp, core, 1, keepdims=False)
    chip_sum = (mine + lax.ppermute(theirs, "tp", swap).astype(F32)).astype(BF16)
    same_core = [list(range(c, tp, 2)) for c in range(2)]
    arrived = lax.all_to_all(chip_sum, "tp", 0, 0, tiled=True, axis_index_groups=same_core)
    mlp_own = arrived.astype(F32).sum(axis=0)
    lcb_own = lax.dynamic_slice_in_dim(got[:, feat : feat + fmw], me * own, own, 1)
    lcb_own = lcb_own.astype(F32).T * (1.0 / LCB_SCALE)
    mix = jnp.concatenate([mlp_own, lcb_own], axis=0)
    own_mean = jnp.mean(mix, axis=0)
    delta = mix - own_mean
    own_dev = jnp.sum(delta * delta, axis=0)
    own_g = jnp.sum(gg, axis=0)
    own_gd = jnp.sum(gg * delta, axis=0)
    stats = jnp.stack([own_mean, own_dev, own_g, own_gd])
    message = jnp.concatenate([delta[:own].astype(BF16), *high_low(stats)], axis=0)
    every = lax.all_gather(message, "tp", axis=0, tiled=False)
    numbers = every[:, own : own + 4].astype(F32) + every[:, own + 4 :].astype(F32)
    means, devs, gs, gds = (numbers[:, k] for k in range(4))
    full = width * tp
    mean = jnp.mean(means, axis=0)
    shift = means - mean
    var = (jnp.sum(devs, axis=0) + width * jnp.sum(shift * shift, axis=0)) / full
    rstd = 1.0 / jnp.sqrt(var + 1e-05)
    first = jnp.sum(gs, axis=0) / full
    second = jnp.sum(gds + shift * gs, axis=0) * rstd / full
    block = (delta + (own_mean - mean)) * rstd * output_norm_gain[:, None]
    block_result = block.astype(BF16).T
    gg_all = (
        got[:, feat + fmw :]
        .reshape(tp, 3, 8, 2, group_rows)
        .transpose(0, 1, 3, 2, 4)
        .reshape(tp, own, group_rows)
    )
    xhat = (every[:, :own].astype(F32) + shift[:, None]) * rstd
    dmix = ((gg_all.astype(F32) * (1.0 / GG_SCALE) - first - xhat * second) * rstd).astype(BF16)
    dmix = dmix.reshape(fmw, group_rows)
    grad = jnp.einsum("sh,cs->hc", hidden, dmix, preferred_element_type=F32).astype(BF16)
    parts = lax.all_to_all(grad.reshape(dp, -1, fmw), "dp", 0, 0, tiled=True)
    return (block_result, parts.astype(F32).sum(axis=0))


def solution(mesh):
    return jax.shard_map(
        on_device,
        mesh=mesh,
        in_specs=(
            P(("dp", "tp"), None, None),
            P(),
            P(),
            P(None, "tp"),
            P("tp", None),
            P("tp"),
            P("dp", "tp"),
        ),
        out_specs=(P("dp", "tp"), P(("tp", "dp"), None)),
        check_vma=False,
    )
```

profile of v0, /device:TPU:8, one launch (start us, length us, event | category | flops | bytes accessed | tf_op | source)
XLA Modules:
  0.0 120.3 jit_solution(396855091383316326)
XLA Ops:
  0.6 0.0 copy-start
  0.7 1.6 %copy-done = bf16[24,192,256]{2,1,0:T(8,128)(2,1)S(1)} copy-done((bf16[24,192,256]{2,1,0:T(8,128)(2,1)S(1)}, bf16[24,192,256]{2,1,0:T(8,128)(2,1)}, u32[]{:S(2)}) %copy-start) | copy-done | bytes 2359320
  2.3 1.4 %fusion.8 = f16[24,4,192]{2,1,0:T(4,128)(2,1)S(1)} fusion(bf16[24,192,256]{2,1,0:T(8,128)(2,1)S(1)} %copy-done, bf16[256,4]{0,1:T(4,128)(2,1)} %param.9), kind=kOutput, calls=%fused_computation.15 | convolution fusion | flops 9474048 | bytes 2398208 | tf_op jit(solution)/shard_map/sef,fj->sje/dot_general | solution.py:34
  3.7 0.1 convert_element_type.84
  3.9 0.0 copy-done.7
  3.9 0.1 fusion.19
  4.0 0.0 copy-done.9
  4.0 1.1 fusion.33
  5.1 0.4 multiply_reduce_fusion
  5.5 0.2 copy.52
  5.8 0.1 multiply_convert_fusion
  5.9 0.1 pad_maximum_fusion
  6.0 0.0 copy-start.11
  6.0 38.7 %all-gather.2 = f16[384,5632]{1,0:T(8,128)(2,1)S(1)} all-gather(f16[24,5632]{1,0:T(8,128)(2,1)S(1)} %pad_maximum_fusion), channel_id=1, replica_groups=mesh['dp'=32,'tp'=16] {'tp'}, dimensions={0}, use_global_device_ids=true | all-gather | bytes 4595712 | tf_op jit(solution)/shard_map/all_gather | solution.py:46
  44.7 0.0 copy-done.11
  44.7 1.0 fusion.17
  45.8 0.9 copy-done.1
  46.7 0.7 copy-done.2
  47.4 0.0 copy-done.6
  47.4 0.3 convolution_bitcast_fusion
  47.7 1.4 %copy.40 = f32[768,384]{1,0:T(8,128)} copy(f32[768,384]{0,1:T(8,128)S(1)} %convolution_bitcast_fusion) | data formatting | bytes 2359296 | tf_op jit(solution)/shard_map/hc,sh->cs/dot_general | solution.py:49
  49.1 1.1 fusion.18
  50.2 2.3 %collective-permute-start = (bf16[8,48,384]{2,1,0:T(8,128)(2,1)S(1)}, bf16[8,48,384]{2,1,0:T(8,128)(2,1)S(1)}, u32[]{:S(2)}, u32[]{:S(2)}) collective-permute-start(bf16[8,48,384]{2,1,0:T(8,128)(2,1)S(1)} %fusion.18), channel_id=1, source_target_pairs={{0,1},{1,0},{2,3},{3,2},{4,5},{5,4},{6,7},{7,6},{8,9},{9,8},{10,11... | collective-permute-start | bytes 884744 | tf_op jit(solution)/shard_map/ppermute | solution.py:54
  52.5 0.0 slice-start
  52.5 1.2 collective-permute-done
  53.7 1.9 %fusion.9 = bf16[8,48,384]{2,1,0:T(8,128)(2,1)} fusion(bf16[8,48,384]{2,1,0:T(8,128)(2,1)S(1)} %collective-permute-done, f32[8,2,48,384]{3,2,1,0:T(8,128)} %bitcast.76, s32[]{:T(128)S(6)} %select_n.18), kind=kLoop, calls=%fused_computation.21 | loop fusion | flops 442368 | bytes 1179652 | tf_op jit(solution)/shard_map/convert_element_type | solution.py:54
  55.5 4.1 %all-to-all-start = ((bf16[8,48,384]{2,1,0:T(8,128)(2,1)}), bf16[8,48,384]{2,1,0:T(8,128)(2,1)}, u32[]{:S(2)}, u32[]{:S(2)}) async-start(bf16[8,48,384]{2,1,0:T(8,128)(2,1)} %fusion.9), calls=%async_computation | async-start | bytes 589824 | tf_op jit(solution)/shard_map/all_to_all | solution.py:56
  59.6 0.0 slice-done
  59.6 0.1 constant_dynamic-slice_fusion
  59.8 0.7 copy.47
  60.5 1.2 convert_multiply_fusion
  61.7 1.6 %mul.195 = f32[16,3,8,2,384]{4,3,2,1,0:T(2,128)} reshape(f32[384,768]{1,0:T(8,128)S(1)} %convert_multiply_fusion) | data formatting | bytes 2359296 | tf_op jit(solution)/shard_map/mul | solution.py:87
  63.3 1.4 %copy.43 = f32[16,3,2,8,384]{4,3,2,1,0:T(8,128)S(1)} copy(f32[16,3,2,8,384]{4,2,3,1,0:T(2,128)} %bitcast.74) | data formatting | bytes 2359296 | tf_op jit(solution)/shard_map/mul | solution.py:87
  64.7 0.6 fusion.24
  65.3 7.7 %all-to-all-done = bf16[8,48,384]{2,1,0:T(8,128)(2,1)} async-done(((bf16[8,48,384]{2,1,0:T(8,128)(2,1)}), bf16[8,48,384]{2,1,0:T(8,128)(2,1)}, u32[]{:S(2)}, u32[]{:S(2)}) %all-to-all-start) | async-done | bytes 294944 | tf_op jit(solution)/shard_map/all_to_all | solution.py:56
  73.0 1.1 convert_reduce_fusion.1
  74.1 1.0 multiply_reduce_fusion.2
  75.2 16.6 %all-gather = bf16[896,384]{1,0:T(8,128)(2,1)S(1)} all-gather(bf16[56,384]{1,0:T(8,128)(2,1)S(1)} %pad_maximum_fusion.1), channel_id=2, replica_groups=mesh['dp'=32,'tp'=16] {'tp'}, dimensions={0}, use_global_device_ids=true | all-gather | bytes 731136 | tf_op jit(solution)/shard_map/all_gather | solution.py:68
  91.8 0.1 slice_reduce_fusion.1
  92.0 0.0 copy-done.4
  92.0 0.0 copy-start.3
  92.0 0.3 fusion.5
  92.3 0.6 copy-done.3
  92.9 1.1 fusion.1
  94.1 10.2 %all-to-all-start.1 = ((bf16[32,8,768]{2,1,0:T(8,128)(2,1)}), bf16[32,8,768]{2,1,0:T(8,128)(2,1)S(1)}, u32[]{:S(2)}, u32[]{:S(2)}) async-start(bf16[32,8,768]{2,1,0:T(8,128)(2,1)} %fusion.1), calls=%async_computation.1 | async-start | bytes 786432 | tf_op jit(solution)/shard_map/all_to_all | solution.py:90
  104.3 0.7 fusion.21
  105.0 14.7 %all-to-all-done.1 = bf16[32,8,768]{2,1,0:T(8,128)(2,1)S(1)} async-done(((bf16[32,8,768]{2,1,0:T(8,128)(2,1)}), bf16[32,8,768]{2,1,0:T(8,128)(2,1)S(1)}, u32[]{:S(2)}, u32[]{:S(2)}) %all-to-all-start.1) | async-done | bytes 393248 | tf_op jit(solution)/shard_map/all_to_all | solution.py:90
  119.7 0.7 convert_reduce_fusion
  (28 shorter events, 0.2 us)
Async XLA Ops:
  0.6 1.7 %copy-start = (bf16[24,192,256]{2,1,0:T(8,128)(2,1)S(1)}, bf16[24,192,256]{2,1,0:T(8,128)(2,1)}, u32[]{:S(2)}) copy-start(bf16[24,192,256]{2,1,0:T(8,128)(2,1)} %param.7) | copy-start | bytes 7077892
  2.3 1.6 %copy-start.7 = (bf16[384,96]{0,1:T(8,128)(2,1)S(1)}, bf16[384,96]{0,1:T(8,128)(2,1)}, u32[]{:S(2)}) copy-start(bf16[384,96]{0,1:T(8,128)(2,1)} %param.13) | copy-start | bytes 221188
  2.3 1.6 %copy-start.10 = (f32[96]{0:T(128)S(1)}, f32[96]{0:T(128)}, u32[]{:S(2)}) copy-start(f32[96]{0:T(128)} %param.12) | copy-start | bytes 1156
  2.3 1.7 %copy-start.9 = (bf16[256,16]{0,1:T(8,128)(2,1)S(1)}, bf16[256,16]{0,1:T(8,128)(2,1)}, u32[]{:S(2)}) copy-start(bf16[256,16]{0,1:T(8,128)(2,1)} %param.8) | copy-start | bytes 24580
  6.0 38.7 %copy-start.11 = (bf16[4096,256]{1,0:T(8,128)(2,1)S(1)}, bf16[4096,256]{1,0:T(8,128)(2,1)}, u32[]{:S(2)}) copy-start(bf16[4096,256]{1,0:T(8,128)(2,1)} %param.10) | copy-start | bytes 6291460
  44.7 2.0 %copy-start.1 = (f16[384,5632]{1,0:T(8,128)(2,1)}, f16[384,5632]{1,0:T(8,128)(2,1)S(1)}, u32[]{:S(2)}) copy-start(f16[384,5632]{1,0:T(8,128)(2,1)S(1)} %all-gather.2) | copy-start | bytes 12976132
  44.7 2.7 %copy-start.6 = (bf16[256,768]{1,0:T(8,128)(2,1)S(1)}, bf16[256,768]{1,0:T(8,128)(2,1)}, u32[]{:S(2)}) copy-start(bf16[256,768]{1,0:T(8,128)(2,1)} %param.11) | copy-start | bytes 1179652
  46.7 0.7 copy-start.2
  50.2 3.5 %collective-permute-start = (bf16[8,48,384]{2,1,0:T(8,128)(2,1)S(1)}, bf16[8,48,384]{2,1,0:T(8,128)(2,1)S(1)}, u32[]{:S(2)}, u32[]{:S(2)}) collective-permute-start(bf16[8,48,384]{2,1,0:T(8,128)(2,1)S(1)} %fusion.18), channel_id=1, source_target_pairs={{0,1},{1,0},{2,3},{3,2},{4,5},{5,4},{6,7},{7,6},{8,9},{9,8},{10,11... | collective-permute-start | bytes 884744 | tf_op jit(solution)/shard_map/ppermute | solution.py:54
  52.5 7.1 %slice-start = ((f16[384,5632]{1,0:T(8,128)(2,1)}), f16[384,768]{1,0:T(8,128)(2,1)S(1)}, s32[]{:S(2)}) async-start(f16[384,5632]{1,0:T(8,128)(2,1)} %copy-done.1), calls=%async_computation.2 | async-start | bytes 1179648 | tf_op jit(solution)/shard_map/slice | solution.py:58
  55.5 17.5 %all-to-all-start = ((bf16[8,48,384]{2,1,0:T(8,128)(2,1)}), bf16[8,48,384]{2,1,0:T(8,128)(2,1)}, u32[]{:S(2)}, u32[]{:S(2)}) async-start(bf16[8,48,384]{2,1,0:T(8,128)(2,1)} %fusion.9), calls=%async_computation | async-start | bytes 589824 | tf_op jit(solution)/shard_map/all_to_all | solution.py:56
  63.3 1.4 %copy-start.8 = (f16[384,48]{0,1:T(8,128)(2,1)S(1)}, f16[384,48]{0,1:T(8,128)(2,1)}, u32[]{:S(2)}) copy-start(f16[384,48]{0,1:T(8,128)(2,1)} %copy.47) | copy-start | bytes 110596
  75.1 16.9 %copy-start.4 = (f32[96,384]{1,0:T(8,128)}, f32[96,384]{1,0:T(8,128)S(1)}, u32[]{:S(2)}) copy-start(f32[96,384]{1,0:T(8,128)S(1)} %get-tuple-element.15) | copy-start | bytes 442372
  92.0 0.9 copy-start.3
  92.3 11.9 %copy-start.5 = (f32[96,384]{1,0:T(8,128)S(1)}, f32[96,384]{1,0:T(8,128)}, u32[]{:S(2)}) copy-start(f32[96,384]{1,0:T(8,128)} %copy-done.4) | copy-start | bytes 442372
  94.1 25.6 %all-to-all-start.1 = ((bf16[32,8,768]{2,1,0:T(8,128)(2,1)}), bf16[32,8,768]{2,1,0:T(8,128)(2,1)S(1)}, u32[]{:S(2)}, u32[]{:S(2)}) async-start(bf16[32,8,768]{2,1,0:T(8,128)(2,1)} %fusion.1), calls=%async_computation.1 | async-start | bytes 786432 | tf_op jit(solution)/shard_map/all_to_all | solution.py:90
where the time goes:
time: 121 us; the launch traced here: 120 us
  blocking collectives  55.3 us (46%)
  waiting for transfers between devices  23.5 us (19%)
  starting transfers between devices  16.5 us (14%)
  local copies, waits for them, and re-layouts  10.6 us (9%)
  other arithmetic  8.4 us (7%)
  matrix products  5.05 us (4%)
    all_gather x1, blocking collectives, on_device(): got = lax.all_gather(sent, 'tp', axis=0, tiled=True)  38.7 us
    all_gather x1, blocking collectives, on_device(): every = lax.all_gather(message, 'tp', axis=0, tiled=False)  16.6 us
    all_to_all x1, waiting for transfers between devices, on_device(): parts = lax.all_to_all(grad.reshape(dp, -1, fmw), 'dp', 0, 0, tiled=True)  14.7 us
    all_to_all x1, starting transfers between devices, on_device(): parts = lax.all_to_all(grad.reshape(dp, -1, fmw), 'dp', 0, 0, tiled=True)  10.2 us
    all_to_all x1, waiting for transfers between devices, on_device(): lax.all_to_all(chip_sum, 'tp', 0, 0, tiled=True, axis_index_groups=same_c...  7.68 us
    unnamed x26, local copies, waits for them, and re-layouts  4.87 us
    all_to_all x1, starting transfers between devices, on_device(): lax.all_to_all(chip_sum, 'tp', 0, 0, tiled=True, axis_index_groups=same_c...  4.06 us
    mul x2, local copies, waits for them, and re-layouts, on_device(): gg_all.astype(F32) * (1.0 / GG_SCALE) - first - xhat * second  2.98 us
  transfers between devices with their start and end apart: 3, of which 3 were waited for; matrix products, arithmetic and copies ran while one was open for 5% of the time, Pallas kernels for 0%

commit v1 on v0

--- a/solution.py
+++ b/solution.py
@@ -43,7 +43,9 @@
         .reshape(samples, -1)
     )
     sent = jnp.concatenate([normed, (lcb * LCB_SCALE).astype(F16), gg_packed], axis=1)
-    got = lax.all_gather(sent, "tp", axis=0, tiled=True)
+    got = jnp.concatenate(
+        lax.all_to_all(jnp.stack([sent] * lax.axis_size("tp")), "tp", 0, 0), axis=0
+    )
     pre = jnp.dot(got[:, :feat].astype(BF16), w_up, preferred_element_type=F32)
     hidden = jax.nn.gelu(pre * (1.0 / NORMED_SCALE), approximate=True).astype(BF16)
     mlp = jnp.einsum("hc,sh->cs", w_down, hidden, preferred_element_type=F32)

time: 121 us -> 196 us (1.62)
  waiting for transfers between devices: 23.5 us -> 119 us
  blocking collectives: 55.3 us -> 16.6 us
  starting transfers between devices: 16.5 us -> 27.2 us
  local copies, waits for them, and re-layouts: 10.6 us -> 14.6 us
  matrix products: 5.05 us -> 7.62 us
    all_to_all x0 -> x1, waiting for transfers between devices: none -> 97.1 us  [on_device(): lax.all_to_all(jnp.stack([sent] * lax.axis_size('tp')), 'tp', 0, 0)]
    all_gather x1 -> x0, blocking collectives: 38.7 us -> none  [on_device(): got = lax.all_gather(sent, 'tp', axis=0, tiled=True)]
    all_to_all x0 -> x1, starting transfers between devices: none -> 10.5 us  [on_device(): lax.all_to_all(jnp.stack([sent] * lax.axis_size('tp')), 'tp', 0, 0)]
    dot_general x1, matrix products: 1.05 us -> 3.63 us  [on_device(): pre = jnp.dot(got[:, :feat].astype(BF16), w_up, preferred_element_type=F32)]
    another operation x0 -> x1, local copies, waits for them, and re-layouts: none -> 2.29 us  [on_device(): jnp.stack([sent] * lax.axis_size('tp'))]
    unnamed x26 -> x22, local copies, waits for them, and re-layouts: 4.87 us -> 2.82 us
    slice x2 -> x1, local copies, waits for them, and re-layouts: 0.01 us -> 2.02 us  [on_device(): got[:, feat:feat + fmw]]
  transfers between devices with their start and end apart: 3 -> 4, of which waited for: 3 -> 3; matrix products, arithmetic and copies ran while one was open for 5% -> 5% of each run, Pallas kernels for 0% -> 0%
where the time goes in v1:
time: 196 us; the launch traced here: 195 us
  waiting for transfers between devices  119 us (61%)
  starting transfers between devices  27.2 us (14%)
  blocking collectives  16.6 us (8%)
  local copies, waits for them, and re-layouts  14.6 us (7%)
  other arithmetic  9.31 us (5%)
  matrix products  7.62 us (4%)
    all_to_all x1, waiting for transfers between devices, on_device(): lax.all_to_all(jnp.stack([sent] * lax.axis_size('tp')), 'tp', 0, 0)  97.1 us
    all_gather x1, blocking collectives, on_device(): every = lax.all_gather(message, 'tp', axis=0, tiled=False)  16.6 us
    all_to_all x1, waiting for transfers between devices, on_device(): parts = lax.all_to_all(grad.reshape(dp, -1, fmw), 'dp', 0, 0, tiled=True)  14.7 us
    all_to_all x1, starting transfers between devices, on_device(): lax.all_to_all(jnp.stack([sent] * lax.axis_size('tp')), 'tp', 0, 0)  10.5 us
    all_to_all x1, starting transfers between devices, on_device(): parts = lax.all_to_all(grad.reshape(dp, -1, fmw), 'dp', 0, 0, tiled=True)  10.2 us
    all_to_all x1, waiting for transfers between devices, on_device(): lax.all_to_all(chip_sum, 'tp', 0, 0, tiled=True, axis_index_groups=same_c...  6.76 us
    all_to_all x1, starting transfers between devices, on_device(): lax.all_to_all(chip_sum, 'tp', 0, 0, tiled=True, axis_index_groups=same_c...  4.69 us
  transfers between devices with their start and end apart: 4, of which 3 were waited for; matrix products, arithmetic and copies ran while one was open for 5% of the time, Pallas kernels for 0%

profile of v1, /device:TPU:8, one launch (start us, length us, event | category | flops | bytes accessed | tf_op | source)
XLA Modules:
  0.0 194.8 jit_solution(2700624138864377551)
XLA Ops:
  0.6 0.0 copy-start
  0.6 1.1 fusion.19
  1.8 0.6 copy-done
  2.4 1.4 fusion.8
  3.8 0.1 convert_element_type.84
  3.9 0.0 copy-done.8
  3.9 1.1 fusion.32
  5.0 0.2 copy.29
  5.3 0.4 multiply_reduce_fusion
  5.7 0.1 multiply_convert_fusion
  5.8 0.1 pad_maximum_fusion
  5.9 2.3 %stack.10 = f16[16,24,5632]{2,1,0:T(8,128)(2,1)} broadcast(f16[24,5632]{1,0:T(8,128)(2,1)S(1)} %pad_maximum_fusion), dimensions={1,2} | broadcast | bytes 4595712 | tf_op jit(solution)/shard_map/stack | solution.py:47
  8.2 10.5 %all-to-all-start = ((f16[16,24,5632]{2,1,0:T(8,128)(2,1)}), f16[16,24,5632]{2,1,0:T(8,128)(2,1)}, u32[]{:S(2)}, u32[]{:S(2)}) async-start(f16[16,24,5632]{2,1,0:T(8,128)(2,1)} %stack.10), calls=%async_computation | async-start | bytes 8650752 | tf_op jit(solution)/shard_map/all_to_all | solution.py:47
  18.7 97.1 %all-to-all-done = f16[16,24,5632]{2,1,0:T(8,128)(2,1)} async-done(((f16[16,24,5632]{2,1,0:T(8,128)(2,1)}), f16[16,24,5632]{2,1,0:T(8,128)(2,1)}, u32[]{:S(2)}, u32[]{:S(2)}) %all-to-all-start) | async-done | bytes 4325408 | tf_op jit(solution)/shard_map/all_to_all | solution.py:47
  115.8 3.6 %fusion.17 = bf16[384,256]{1,0:T(8,128)(2,1)S(1)} fusion(bf16[4096,256]{1,0:T(8,128)(2,1)} %param.10, f16[384,5632]{1,0:T(8,128)(2,1)} %bitcast.7), kind=kOutput, calls=%fused_computation.30 | convolution fusion | flops 807862272 | bytes 5439488 | tf_op jit(solution)/shard_map/dot_general | solution.py:49
  119.4 0.0 copy-start.2
  119.4 0.7 copy-done.2
  120.1 0.0 copy-done.6
  120.1 0.3 convolution_bitcast_fusion
  120.4 1.4 copy.19
  121.8 1.9 fusion.18
  123.7 1.9 collective-permute-start
  125.6 2.0 %slice.51 = f16[384,768]{1,0:T(8,128)(2,1)} slice(f16[384,5632]{1,0:T(8,128)(2,1)} %bitcast.7), slice={[0:384], [4096:4864]} | slice | bytes 1179648 | tf_op jit(solution)/shard_map/slice | solution.py:60
  127.6 0.0 collective-permute-done
  127.6 0.0 copy-done.1
  127.6 1.7 fusion.9
  129.4 4.7 %all-to-all-start.1 = ((bf16[8,48,384]{2,1,0:T(8,128)(2,1)}), bf16[8,48,384]{2,1,0:T(8,128)(2,1)}, u32[]{:S(2)}, u32[]{:S(2)}) async-start(bf16[8,48,384]{2,1,0:T(8,128)(2,1)} %fusion.9), calls=%async_computation.1 | async-start | bytes 589824 | tf_op jit(solution)/shard_map/all_to_all | solution.py:58
  134.1 1.0 constant_dynamic-slice_fusion
  135.1 0.7 copy.26
  135.9 1.2 convert_multiply_fusion
  137.0 1.6 mul.195
  138.7 1.4 copy.22
  140.0 0.0 copy-done.7
  140.0 0.6 fusion.24
  140.7 6.8 %all-to-all-done.1 = bf16[8,48,384]{2,1,0:T(8,128)(2,1)} async-done(((bf16[8,48,384]{2,1,0:T(8,128)(2,1)}), bf16[8,48,384]{2,1,0:T(8,128)(2,1)}, u32[]{:S(2)}, u32[]{:S(2)}) %all-to-all-start.1) | async-done | bytes 294944 | tf_op jit(solution)/shard_map/all_to_all | solution.py:58
  147.4 1.1 convert_reduce_fusion.1
  148.5 0.0 copy-done.9
  148.5 1.0 multiply_reduce_fusion.2
  149.6 16.6 %all-gather = bf16[896,384]{1,0:T(8,128)(2,1)S(1)} all-gather(bf16[56,384]{1,0:T(8,128)(2,1)S(1)} %pad_maximum_fusion.1), channel_id=2, replica_groups=mesh['dp'=32,'tp'=16] {'tp'}, dimensions={0}, use_global_device_ids=true | all-gather | bytes 731136 | tf_op jit(solution)/shard_map/all_gather | solution.py:70
  166.2 0.1 slice_reduce_fusion.1
  166.4 0.0 copy-done.4
  166.4 0.3 fusion.5
  166.8 0.6 copy-done.3
  167.4 1.1 fusion.1
  168.5 10.2 %all-to-all-start.2 = ((bf16[32,8,768]{2,1,0:T(8,128)(2,1)}), bf16[32,8,768]{2,1,0:T(8,128)(2,1)S(1)}, u32[]{:S(2)}, u32[]{:S(2)}) async-start(bf16[32,8,768]{2,1,0:T(8,128)(2,1)} %fusion.1), calls=%async_computation.2 | async-start | bytes 786432 | tf_op jit(solution)/shard_map/all_to_all | solution.py:92
  178.7 0.7 fusion.21
  179.4 14.7 %all-to-all-done.2 = bf16[32,8,768]{2,1,0:T(8,128)(2,1)S(1)} async-done(((bf16[32,8,768]{2,1,0:T(8,128)(2,1)}), bf16[32,8,768]{2,1,0:T(8,128)(2,1)S(1)}, u32[]{:S(2)}, u32[]{:S(2)}) %all-to-all-start.2) | async-done | bytes 393248 | tf_op jit(solution)/shard_map/all_to_all | solution.py:92
  194.1 0.7 convert_reduce_fusion
  (25 shorter events, 0.2 us)
Async XLA Ops:
  0.6 1.7 copy-start
  2.4 1.5 copy-start.8
  8.2 107.6 %all-to-all-start = ((f16[16,24,5632]{2,1,0:T(8,128)(2,1)}), f16[16,24,5632]{2,1,0:T(8,128)(2,1)}, u32[]{:S(2)}, u32[]{:S(2)}) async-start(f16[16,24,5632]{2,1,0:T(8,128)(2,1)} %stack.10), calls=%async_computation | async-start | bytes 8650752 | tf_op jit(solution)/shard_map/all_to_all | solution.py:47
  115.8 4.3 %copy-start.6 = (bf16[256,768]{1,0:T(8,128)(2,1)S(1)}, bf16[256,768]{1,0:T(8,128)(2,1)}, u32[]{:S(2)}) copy-start(bf16[256,768]{1,0:T(8,128)(2,1)} %param.11) | copy-start | bytes 1179652
  119.4 0.7 copy-start.2
  121.8 5.9 %copy-start.1 = (f32[768,384]{1,0:T(8,128)S(1)}, f32[768,384]{1,0:T(8,128)}, u32[]{:S(2)}) copy-start(f32[768,384]{1,0:T(8,128)} %copy.19) | copy-start | bytes 3538948
  123.7 4.0 %collective-permute-start = (bf16[8,48,384]{2,1,0:T(8,128)(2,1)}, bf16[8,48,384]{2,1,0:T(8,128)(2,1)}, u32[]{:S(2)}, u32[]{:S(2)}) collective-permute-start(bf16[8,48,384]{2,1,0:T(8,128)(2,1)} %fusion.18), channel_id=1, source_target_pairs={{0,1},{1,0},{2,3},{3,2},{4,5},{5,4},{6,7},{7,6},{8,9},{9,8},{10,11... | collective-permute-start | bytes 884744 | tf_op jit(solution)/shard_map/ppermute | solution.py:56
  129.4 18.1 %all-to-all-start.1 = ((bf16[8,48,384]{2,1,0:T(8,128)(2,1)}), bf16[8,48,384]{2,1,0:T(8,128)(2,1)}, u32[]{:S(2)}, u32[]{:S(2)}) async-start(bf16[8,48,384]{2,1,0:T(8,128)(2,1)} %fusion.9), calls=%async_computation.1 | async-start | bytes 589824 | tf_op jit(solution)/shard_map/all_to_all | solution.py:58
  138.7 1.4 copy-start.7
  138.7 9.9 %copy-start.9 = (f32[96]{0:T(128)S(1)}, f32[96]{0:T(128)}, u32[]{:S(2)}) copy-start(f32[96]{0:T(128)} %param.12) | copy-start | bytes 1156
  149.5 16.9 %copy-start.4 = (f32[96,384]{1,0:T(8,128)}, f32[96,384]{1,0:T(8,128)S(1)}, u32[]{:S(2)}) copy-start(f32[96,384]{1,0:T(8,128)S(1)} %get-tuple-element.15) | copy-start | bytes 442372
  166.4 0.9 copy-start.3
  166.8 11.9 %copy-start.5 = (f32[96,384]{1,0:T(8,128)S(1)}, f32[96,384]{1,0:T(8,128)}, u32[]{:S(2)}) copy-start(f32[96,384]{1,0:T(8,128)} %copy-done.4) | copy-start | bytes 442372
  168.5 25.6 %all-to-all-start.2 = ((bf16[32,8,768]{2,1,0:T(8,128)(2,1)}), bf16[32,8,768]{2,1,0:T(8,128)(2,1)S(1)}, u32[]{:S(2)}, u32[]{:S(2)}) async-start(bf16[32,8,768]{2,1,0:T(8,128)(2,1)} %fusion.1), calls=%async_computation.2 | async-start | bytes 786432 | tf_op jit(solution)/shard_map/all_to_all | solution.py:92
